TPU v7x, 32 devices: a whole 2x2x4 slice. The times are simulated.
32 devices in a mesh: row: 8 (over y, x, core), col: 4 (over z).
Axes of the slice: x: 2, y: 2, z: 4, core: 2. Of those that a mesh axis runs over, the one named last changes fastest.
Arguments:
- matrix: float32 [61440, 1536], P('row', 'col'), may hold values from -1 to 96, as said below
Outputs:
- stepped: float32 [61440, 1536], P('row', 'col')
Inputs may be any that keep to these rules, and one draw needn't show every extreme that they name: `matrix`: entries where global row equals global column lie in 64 to 96; all other entries lie in -1 to 1, so the symmetrized first diagonal tile is positive definite.
All inputs are finite; a program needn't handle non-finite values.
Results may differ from a plain program's by a relative error of at most 0.0003.
Values sent between devices are 32-bit elements; how exact they have to be, the bound alone decides.
A program may use at most 64 MiB of HBM per device.

v0:
```python
import functools

import jax
import jax.numpy as jnp
from jax import lax
from jax.experimental import pallas as pl
from jax.experimental.pallas import tpu as pltpu
from jax.sharding import PartitionSpec as P

B = 64
R = 256
H = R // 2
LANES = 128
GROUP = 4
SPLIT = 2
S = H // SPLIT
LEAD = 6
EARLY = 2
MESH = pl.DeviceIdType.MESH
HI = lax.Precision.HIGHEST


def mm(a, b, contract):
    return lax.dot_general(
        a, b, ((contract[:1], contract[1:]), ((), ())), precision=HI, preferred_element_type=jnp.float32
    )


def kernel(n_row, n_col, a_ref, a_v, pack, corner_b, cols_b, m_b, head,
           a_in, f_send, f_recv, k_send, k_recv, c_send, c_recv):
    p = lax.axis_index("row")
    q = lax.axis_index("col")
    rows, width = a_v.shape
    n = rows // R
    per = n_row // n_col
    last = n_col - 1

    def fetch(c):
        at = pl.ds(pl.multiple_of(c * R, R), R)
        return pltpu.make_async_copy(a_ref.at[at], a_v.at[at], a_in.at[c])

    def hop(c):
        at = pl.ds(pl.multiple_of(c * S, S), S)
        return pltpu.make_async_remote_copy(
            src_ref=pack.at[at], dst_ref=pack.at[at], send_sem=f_send.at[c], recv_sem=f_recv.at[c],
            device_id=(p, lax.rem(q + 1, n_col)), device_id_type=MESH,
        )

    def peer(i):
        return lax.rem(p + i, n_row), q

    def send_corner(i):
        return pltpu.make_async_remote_copy(
            src_ref=pack.at[pl.ds(0, B)], dst_ref=corner_b, send_sem=k_send.at[i - 1], recv_sem=k_recv.at[0],
            device_id=peer(i), device_id_type=MESH,
        )

    def send_cols(i, slot):
        return pltpu.make_async_remote_copy(
            src_ref=pack.at[pl.ds(0, H)], dst_ref=cols_b.at[slot], send_sem=c_send.at[i - 1],
            recv_sem=c_recv.at[slot], device_id=peer(i), device_id_type=MESH,
        )

    barrier = pltpu.get_barrier_semaphore()

    @pl.when(q > 0)
    def _():
        pl.semaphore_signal(barrier, inc=1, device_id=(p, q - 1), device_id_type=MESH)

    for i in range(1, n_row):
        pl.semaphore_signal(barrier, inc=1, device_id=peer(i), device_id_type=MESH)

    @pl.when(q < last)
    def _():
        pl.semaphore_signal(barrier, inc=1, device_id=(p, q + 1), device_id_type=MESH)

    early = min(EARLY, n)
    for c in range(early):
        fetch(c).start()

    ends = jnp.where(q > 0, 1, 0) + jnp.where(q < last, 1, 0)
    pl.semaphore_wait(barrier, n_row - 1 + ends)

    lane = lax.broadcasted_iota(jnp.int32, (H, LANES), 1)

    def source(c):
        fetch(c).wait()
        base = pl.multiple_of(c * R, R)
        top = a_v[pl.ds(base, H), :LANES]
        low = a_v[pl.ds(base + H, H), :LANES]
        pack[pl.ds(pl.multiple_of(c * H, H), H), :] = jnp.where(lane < B, top, pltpu.roll(low, B, 1))
        for part in range(SPLIT):
            hop(c * SPLIT + part).start()

    def forward(h):
        @pl.when(q > 0)
        def _():
            hop(h).wait_recv()

            @pl.when(q < last)
            def _():
                hop(h).start()

    parts = n * SPLIT
    sent = 0

    def advance(count):
        nonlocal sent
        for _ in range(min(count, parts - sent)):
            forward(sent)
            sent += 1

    @pl.when(q == 0)
    def _():
        for c in range(early):
            source(c)

    @pl.loop(early, n)
    def _(c):
        fetch(c).start()

    advance(SPLIT)

    @pl.when(q > 0)
    def _():
        fetch(0).wait()

    head[...] = a_v[:B, :]
    mine = p // n_col
    owner = lax.rem(p, n_col) == q

    @pl.when(p == 0)
    def _():
        for i in range(1, n_row):
            send_corner(i).start()
        corner_b[...] = pack[:B, :]

    advance(2)

    @pl.when(owner)
    def _():
        for i in range(1, n_row):
            send_cols(i, mine).start()
        cols_b[mine] = pack[:H, :]

    @pl.when(q == 0)
    def _():
        @pl.loop(early, n)
        def _(c):
            source(c)

    advance(LEAD)

    @pl.when(p != 0)
    def _():
        send_corner(1).wait_recv()

    raw = corner_b[...][:, :B]
    corner = (raw + raw.T) / 2.0
    row64 = lax.broadcasted_iota(jnp.int32, (B, B), 0)
    col64 = lax.broadcasted_iota(jnp.int32, (B, B), 1)
    eye = jnp.where(row64 == col64, 1.0, 0.0)
    aug = jnp.concatenate([corner, eye], axis=1)
    row_id = lax.broadcasted_iota(jnp.int32, (B, 1), 0)
    for k in range(B):
        scale = 1.0 / aug[k:k + 1, k:k + 1]
        weight = jnp.where(row_id > k, aug[:, k:k + 1] * scale, 0.0)
        aug = aug - weight * aug[k:k + 1, :]
        if k % GROUP == GROUP - 1:
            advance(1)
    pivots = jnp.sum(jnp.where(row64 == col64, aug[:, :B], 0.0), axis=1, keepdims=True)
    inv = pltpu.roll(aug, B, 1)[:, :B] / jnp.sqrt(pivots)
    inv_t = inv.T
    advance(1)
    sinv = mm(inv_t, inv, (1, 0))

    for slot in range(per):
        @pl.when(p != q + slot * n_col)
        def _(slot=slot):
            send_cols(1, slot).wait_recv()

    tiles = []
    for j in range(width // B):
        at = j // per * B
        block = cols_b[j % per, at % H:at % H + B, :]
        if at >= H:
            block = pltpu.roll(block, B, 1)
        tiles.append(block[:, :B])
    advance(1)
    m = mm(sinv, jnp.concatenate(tiles, axis=0), (1, 1))
    advance(1)
    first = q == 0
    m_first = jnp.where(first, -inv_t, m[:, :B])
    m = jnp.concatenate([m_first, m[:, B:]], axis=1)
    m_hi = m.astype(jnp.bfloat16)
    m_lo = (m - m_hi.astype(jnp.float32)).astype(jnp.bfloat16)
    m_b[...] = jnp.zeros_like(m_b)
    for i, term in enumerate((m_hi, m_hi, m_lo)):
        m_b[i * LANES:i * LANES + B, :width] = term
        m_b[i * LANES + B:(i + 1) * LANES, width:] = term
    advance(1)
    factor = jnp.where(row64 >= col64, mm(corner, inv_t, (1, 0)), 0.0)
    head[:, :B] = jnp.where(first, factor, head[:, :B])
    wide = lax.broadcasted_iota(jnp.int32, (H, width), 1)
    drop = jnp.logical_and(first, wide < B)

    def update(c):
        @pl.when(jnp.logical_and(q > 0, c > 0))
        def _():
            fetch(c).wait()

        rows_c = pack[pl.ds(pl.multiple_of(c * H, H), H), :]
        hi = rows_c.astype(jnp.bfloat16)
        lo = (rows_c - hi.astype(jnp.float32)).astype(jnp.bfloat16)
        change = jnp.dot(
            jnp.concatenate([hi, lo, hi], axis=1), m_b[...], preferred_element_type=jnp.float32
        )
        base = pl.multiple_of(c * R, R)
        for half in range(2):
            at = pl.ds(base + half * H, H)
            a_v[at, :] = jnp.where(drop, 0.0, a_v[at, :]) - change[:, half * width:(half + 1) * width]

        @pl.when(jnp.logical_and(p == 0, c == 0))
        def _():
            a_v[:B, :] = head[...]

    step = SPLIT // 2
    behind = min(sent // step, (parts - sent) // step)
    caught = behind * step == sent

    @pl.loop(0, behind)
    def _(c):
        for part in range(step):
            forward(sent + c * step + part)
        update(c)

    @pl.loop(behind, n)
    def _(c):
        if caught:
            for part in range(SPLIT):
                forward(c * SPLIT + part)
        update(c)

    @pl.when(q < last)
    def _():
        @pl.loop(0, n * SPLIT)
        def _(c):
            hop(c).wait_send()

    @pl.when(p == 0)
    def _():
        for i in range(1, n_row):
            send_corner(i).wait_send()

    @pl.when(owner)
    def _():
        for i in range(1, n_row):
            send_cols(i, mine).wait_send()


def write_out(x_ref, o_ref, sems):
    n = sems.shape[0]
    step = x_ref.shape[0] // n
    copies = []
    for i in range(n):
        at = pl.ds(i * step, step)
        copies.append(pltpu.make_async_copy(x_ref.at[at], o_ref.at[at], sems.at[i]))
        copies[-1].start()
    for copy in copies:
        copy.wait()


def solution(mesh):
    n_row, n_col = mesh.shape["row"], mesh.shape["col"]

    def step(matrix):
        rows, width = matrix.shape
        n = rows // R
        per = n_row // n_col
        assert rows % R == 0 and n_row % n_col == 0 and width // B // per * B <= R
        updated = pl.pallas_call(
            functools.partial(kernel, n_row, n_col),
            out_shape=jax.ShapeDtypeStruct((rows, width), jnp.float32),
            in_specs=[pl.BlockSpec(memory_space=pltpu.HBM)],
            out_specs=pl.BlockSpec(memory_space=pltpu.VMEM),
            scratch_shapes=[
                pltpu.VMEM((rows // 2, LANES), jnp.float32),
                pltpu.VMEM((B, LANES), jnp.float32),
                pltpu.VMEM((per, H, LANES), jnp.float32),
                pltpu.VMEM((3 * LANES, 2 * width), jnp.bfloat16),
                pltpu.VMEM((B, width), jnp.float32),
                pltpu.SemaphoreType.DMA((n,)),
                pltpu.SemaphoreType.DMA((n * SPLIT,)),
                pltpu.SemaphoreType.DMA((n * SPLIT,)),
                pltpu.SemaphoreType.DMA((n_row - 1,)),
                pltpu.SemaphoreType.DMA((1,)),
                pltpu.SemaphoreType.DMA((n_row - 1,)),
                pltpu.SemaphoreType.DMA((per,)),
            ],
            compiler_params=pltpu.CompilerParams(
                collective_id=0, has_side_effects=True, vmem_limit_bytes=24 * 1024 * 1024
            ),
        )(pltpu.with_memory_space_constraint(matrix, pltpu.HBM))
        return pl.pallas_call(
            write_out,
            out_shape=pltpu.HBM((rows, width), jnp.float32),
            in_specs=[pl.BlockSpec(memory_space=pltpu.VMEM)],
            out_specs=pl.BlockSpec(memory_space=pltpu.HBM),
            scratch_shapes=[pltpu.SemaphoreType.DMA((5,))],
            compiler_params=pltpu.CompilerParams(vmem_limit_bytes=24 * 1024 * 1024),
        )(pltpu.with_memory_space_constraint(updated, pltpu.VMEM))

    return jax.shard_map(
        step, mesh=mesh, in_specs=(P("row", "col"),), out_specs=P("row", "col"), check_vma=False
    )
```

profile of v0, /device:TPU:24, one launch (start us, length us, event | category | flops | bytes accessed | tf_op | source)
XLA Modules:
  0.0 57.1 jit_solution(3248930913176349394)
XLA Ops:
  0.0 52.7 %shard_map.17.x_ref = f32[7680,384]{1,0:T(8,128)S(1)} custom-call(f32[7680,384]{1,0:T(8,128)} %a_ref.1), custom_call_target="tpu_custom_call" | custom-call | tf_op jit(solution)/shard_map/pallas_call | solution.py:281
  52.7 4.4 %shard_map.18 = f32[7680,384]{1,0:T(8,128)} custom-call(f32[7680,384]{1,0:T(8,128)S(1)} %shard_map.17.x_ref), custom_call_target="tpu_custom_call" | custom-call | tf_op jit(solution)/shard_map/pallas_call | solution.py:304
where the time goes:
time: 57.3 us; the launch traced here: 57.1 us
  Pallas kernels  57.1 us (100%)
    pallas_call x1, Pallas kernels, step(): pl.pallas_call(functools.partial(kernel, n_row, n_col), out_shape=jax.Sha...  52.7 us
    pallas_call x1, Pallas kernels, step(): pl.pallas_call(write_out, out_shape=pltpu.HBM((rows, width), jnp.float32)...  4.42 us

commit v1 on v0

--- a/solution.py
+++ b/solution.py
@@ -27,13 +27,17 @@
 
 
 def kernel(n_row, n_col, a_ref, a_v, pack, corner_b, cols_b, m_b, head,
-           a_in, f_send, f_recv, k_send, k_recv, c_send, c_recv):
+           a_in, f_send, b_send, f_recv, k_send, k_recv, c_send, c_recv):
     p = lax.axis_index("row")
     q = lax.axis_index("col")
     rows, width = a_v.shape
     n = rows // R
     per = n_row // n_col
-    last = n_col - 1
+    mid = n_col // 2
+    source_q = jnp.where(q == mid, 0, jnp.where(q > mid, q - 1, q + 1))
+    target_q = jnp.where(q == 0, mid, lax.rem(q + 1, n_col))
+    sends_on = jnp.logical_or(q == 0, jnp.logical_and(q >= mid, q < n_col - 1))
+    sends_back = jnp.logical_and(q > 1, q <= mid)
 
     def fetch(c):
         at = pl.ds(pl.multiple_of(c * R, R), R)
@@ -43,7 +47,14 @@
         at = pl.ds(pl.multiple_of(c * S, S), S)
         return pltpu.make_async_remote_copy(
             src_ref=pack.at[at], dst_ref=pack.at[at], send_sem=f_send.at[c], recv_sem=f_recv.at[c],
-            device_id=(p, lax.rem(q + 1, n_col)), device_id_type=MESH,
+            device_id=(p, target_q), device_id_type=MESH,
+        )
+
+    def hop_back(c):
+        at = pl.ds(pl.multiple_of(c * S, S), S)
+        return pltpu.make_async_remote_copy(
+            src_ref=pack.at[at], dst_ref=pack.at[at], send_sem=b_send.at[c], recv_sem=f_recv.at[c],
+            device_id=(p, lax.rem(q + n_col - 1, n_col)), device_id_type=MESH,
         )
 
     def peer(i):
@@ -65,20 +76,24 @@
 
     @pl.when(q > 0)
     def _():
-        pl.semaphore_signal(barrier, inc=1, device_id=(p, q - 1), device_id_type=MESH)
+        pl.semaphore_signal(barrier, inc=1, device_id=(p, source_q), device_id_type=MESH)
 
     for i in range(1, n_row):
         pl.semaphore_signal(barrier, inc=1, device_id=peer(i), device_id_type=MESH)
 
-    @pl.when(q < last)
-    def _():
-        pl.semaphore_signal(barrier, inc=1, device_id=(p, q + 1), device_id_type=MESH)
+    @pl.when(sends_on)
+    def _():
+        pl.semaphore_signal(barrier, inc=1, device_id=(p, target_q), device_id_type=MESH)
+
+    @pl.when(sends_back)
+    def _():
+        pl.semaphore_signal(barrier, inc=1, device_id=(p, q - 1), device_id_type=MESH)
 
     early = min(EARLY, n)
     for c in range(early):
         fetch(c).start()
 
-    ends = jnp.where(q > 0, 1, 0) + jnp.where(q < last, 1, 0)
+    ends = jnp.where(q > 0, 1, 0) + jnp.where(sends_on, 1, 0) + jnp.where(sends_back, 1, 0)
     pl.semaphore_wait(barrier, n_row - 1 + ends)
 
     lane = lax.broadcasted_iota(jnp.int32, (H, LANES), 1)
@@ -97,9 +112,13 @@
         def _():
             hop(h).wait_recv()
 
-            @pl.when(q < last)
+            @pl.when(sends_on)
             def _():
                 hop(h).start()
+
+            @pl.when(sends_back)
+            def _():
+                hop_back(h).start()
 
     parts = n * SPLIT
     sent = 0
@@ -161,13 +180,20 @@
     col64 = lax.broadcasted_iota(jnp.int32, (B, B), 1)
     eye = jnp.where(row64 == col64, 1.0, 0.0)
     aug = jnp.concatenate([corner, eye], axis=1)
-    row_id = lax.broadcasted_iota(jnp.int32, (B, 1), 0)
+    blocks = [aug[i:i + 8] for i in range(0, B, 8)]
+    row_id = lax.broadcasted_iota(jnp.int32, (8, 1), 0)
     for k in range(B):
-        scale = 1.0 / aug[k:k + 1, k:k + 1]
-        weight = jnp.where(row_id > k, aug[:, k:k + 1] * scale, 0.0)
-        aug = aug - weight * aug[k:k + 1, :]
+        b, at = divmod(k, 8)
+        row = blocks[b][at:at + 1, :]
+        scaled = row / row[:, k:k + 1]
+        for r in range(b, B // 8):
+            weight = blocks[r][:, k:k + 1]
+            if r == b:
+                weight = jnp.where(row_id > at, weight, 0.0)
+            blocks[r] = blocks[r] - weight * scaled
         if k % GROUP == GROUP - 1:
             advance(1)
+    aug = jnp.concatenate(blocks, axis=0)
     pivots = jnp.sum(jnp.where(row64 == col64, aug[:, :B], 0.0), axis=1, keepdims=True)
     inv = pltpu.roll(aug, B, 1)[:, :B] / jnp.sqrt(pivots)
     inv_t = inv.T
@@ -241,11 +267,17 @@
                 forward(c * SPLIT + part)
         update(c)
 
-    @pl.when(q < last)
+    @pl.when(sends_on)
     def _():
         @pl.loop(0, n * SPLIT)
         def _(c):
             hop(c).wait_send()
+
+    @pl.when(sends_back)
+    def _():
+        @pl.loop(0, n * SPLIT)
+        def _(c):
+            hop_back(c).wait_send()
 
     @pl.when(p == 0)
     def _():
@@ -292,6 +324,7 @@
                 pltpu.SemaphoreType.DMA((n,)),
                 pltpu.SemaphoreType.DMA((n * SPLIT,)),
                 pltpu.SemaphoreType.DMA((n * SPLIT,)),
+                pltpu.SemaphoreType.DMA((n * SPLIT,)),
                 pltpu.SemaphoreType.DMA((n_row - 1,)),
                 pltpu.SemaphoreType.DMA((1,)),
                 pltpu.SemaphoreType.DMA((n_row - 1,)),

time: 57.3 us -> 56.5 us (0.986)
  the two profiles are of different devices: /device:TPU:24 before, /device:TPU:8 now
where the time goes in v1:
time: 56.5 us; the launch traced here: 56.4 us
  Pallas kernels  56.4 us (100%)
    pallas_call x1, Pallas kernels, step(): pl.pallas_call(functools.partial(kernel, n_row, n_col), out_shape=jax.Sha...  51.9 us
    pallas_call x1, Pallas kernels, step(): pl.pallas_call(write_out, out_shape=pltpu.HBM((rows, width), jnp.float32)...  4.42 us

profile of v1, /device:TPU:8, one launch (start us, length us, event | category | flops | bytes accessed | tf_op | source)
XLA Modules:
  0.0 56.4 jit_solution(11307751230135473659)
XLA Ops:
  0.0 51.9 %shard_map.17.x_ref = f32[7680,384]{1,0:T(8,128)S(1)} custom-call(f32[7680,384]{1,0:T(8,128)} %a_ref.1), custom_call_target="tpu_custom_call" | custom-call | tf_op jit(solution)/shard_map/pallas_call | solution.py:313
  51.9 4.4 %shard_map.18 = f32[7680,384]{1,0:T(8,128)} custom-call(f32[7680,384]{1,0:T(8,128)S(1)} %shard_map.17.x_ref), custom_call_target="tpu_custom_call" | custom-call | tf_op jit(solution)/shard_map/pallas_call | solution.py:337
